TPU v7x, 32 devices: a whole 2x2x4 slice. The times are simulated.
32 devices in a mesh: blk: 8 (over y, x, core), col: 4 (over z).
Axes of the slice: x: 2, y: 2, z: 4, core: 2. Of those that a mesh axis runs over, the one named last changes fastest.
Arguments:
- tile_u: bfloat16 [8, 16, 1024, 128], P('blk', 'col'), may hold values from -6 to 6
- tile_v: bfloat16 [8, 16, 1024, 128], P('blk', 'col'), may hold values from -6 to 6
- tile_rank: int32 [8, 16], P('blk', 'col'), may hold values from 32 to 128
- panel_u: bfloat16 [16, 1024, 128], P('col', 'blk'), may hold values from -6 to 6
- panel_v: bfloat16 [16, 1024, 128], P('col', 'blk'), may hold values from -0.1875 to 0.1875
- band_rank: int32 [16], P('col'), may hold values from 32 to 128
- row_u: bfloat16 [8, 1024, 128], P('blk', 'col'), may hold values from -6 to 6
- row_v: bfloat16 [8, 1024, 128], P('blk', 'col'), may hold values from -0.5 to 0.5
- row_rank: int32 [8], P('blk'), may hold values from 32 to 128
- target_rank: int32 [8, 16], P('blk', 'col'), may hold values from 32 to 128
Outputs:
- new_u: bfloat16 [8, 16, 1024, 128], P('blk', 'col')
- new_v: bfloat16 [8, 16, 1024, 128], P('blk', 'col')
All inputs are finite; a program needn't handle non-finite values.
Results may differ from a plain program's by a relative error of at most 0.001.
Values may be sent and summed in bfloat16 or wider, within the bound.
A program may use at most 64 MiB of HBM per device.

v0:
```python
import math

import jax
import jax.numpy as jnp
from jax import lax
from jax.sharding import PartitionSpec as P

HIGH = lax.Precision.HIGHEST


def pair_columns(first, second):
    joined = jnp.stack([first, second], axis=-1)
    return joined.reshape(joined.shape[:-2] + (joined.shape[-2] * 2,))


def on_device(
    tile_u, tile_v, tile_rank, panel_u, panel_v, band_rank, row_u, row_v, row_rank, target_rank
):
    width = tile_u.shape[3]
    order = tile_u.shape[2]
    lane = jnp.arange(width)
    row_u_all, row_v_all = (
        lax.all_gather(row_u, "col", axis=1, tiled=True),
        lax.all_gather(row_v, "col", axis=1, tiled=True),
    )
    row_keep = (lane < row_rank[0]).astype(jnp.bfloat16)
    tile_keep = (lane[None, :] < tile_rank[0][:, None]).astype(jnp.bfloat16)
    band_keep = (lane[None, :] < band_rank[:, None]).astype(jnp.bfloat16)
    left_row = row_u_all[0] * row_keep[None, :]
    right_row = row_v_all[0] * row_keep[None, :]
    left_tile = tile_u[0] * tile_keep[:, None, :]
    right_tile = (tile_v[0] * tile_keep[:, None, :]).astype(jnp.float32)
    left = pair_columns(left_tile, jnp.broadcast_to(left_row, left_tile.shape))
    spare = 1.0 - pair_columns(
        tile_keep.astype(jnp.float32),
        jnp.broadcast_to(row_keep.astype(jnp.float32), tile_keep.shape),
    )
    gram = jnp.einsum("jnk,jnl->jkl", left, left, preferred_element_type=jnp.float32)
    gram = gram + spare[:, :, None] * jnp.eye(2 * width, dtype=jnp.float32)[None]
    lower = jnp.linalg.cholesky(gram)
    ortho = lax.linalg.triangular_solve(
        lower, left.astype(jnp.float32), left_side=False, lower=True, transpose_a=True
    )
    target_keep = (lane[None, :] < target_rank[0][:, None]).astype(jnp.float32)
    scale = math.sqrt(order)
    new_u = ortho[:, :, :width] * scale * target_keep[:, None, :]
    head = jnp.transpose(lower, (0, 2, 1))[:, :width, :]
    masked = lax.all_gather(panel_v, "blk", axis=1, tiled=True) * band_keep[:, None, :]
    core = jnp.einsum("nk,jnl->jkl", right_row, masked, preferred_element_type=jnp.float32)
    masked = (lax.all_gather(panel_u, "blk", axis=1, tiled=True) * band_keep[:, None, :]).astype(
        jnp.float32
    )
    panel_part = -jnp.einsum("jnl,jkl->jnk", masked, core, precision=HIGH)
    right = pair_columns(right_tile, panel_part)
    new_v = jnp.einsum("jnc,jmc->jnm", right, head, precision=HIGH)
    new_v = new_v / scale * target_keep[:, None, :]
    return (new_u[None].astype(jnp.bfloat16), new_v[None].astype(jnp.bfloat16))


def solution(mesh):
    return jax.shard_map(
        on_device,
        mesh=mesh,
        in_specs=(
            P("blk", "col", None, None),
            P("blk", "col", None, None),
            P("blk", "col"),
            P("col", "blk", None),
            P("col", "blk", None),
            P("col"),
            P("blk", "col", None),
            P("blk", "col", None),
            P("blk"),
            P("blk", "col"),
        ),
        out_specs=(P("blk", "col", None, None), P("blk", "col", None, None)),
        check_vma=False,
    )
```

profile of v0, /device:TPU:0, one launch (start us, length us, event | category | flops | bytes accessed | tf_op | source)
XLA Modules:
  0.0 317.0 jit_solution(16678338679931156166)
XLA Ops:
  12.1 15.8 %all_gather.12 = bf16[1,1024,128]{2,1,0:T(8,128)(2,1)S(1)} all-gather(bf16[1,256,128]{2,1,0:T(8,128)(2,1)} %param.16), channel_id=1, replica_groups=mesh['blk'=8,'col'=4] {'col'}, dimensions={1}, use_global_device_ids=true | all-gather | bytes 327680 | tf_op jit(solution)/shard_map/all_gather | solution.py:23
  29.5 1.5 copy.74
  31.0 1.5 copy.60
  32.5 1.6 fusion.9
  34.5 2.9 copy.62
  37.4 3.0 copy.63
  41.3 1.3 copy.68
  44.7 1.6 fusion.11
  47.3 46.9 %custom-call.16 = f32[4,128,128]{2,1,0:T(8,128)S(1)} custom-call(f32[4,128,128]{2,1,0:T(8,128)S(1)} %cholesky.122), custom_call_target="Cholesky" | custom-call | tf_op jit(solution)/shard_map/jit(cholesky)/cholesky | solution.py:40
  95.0 40.8 %custom-call.17 = f32[4,1,128,128]{2,3,1,0:T(8,128)} custom-call(f32[4,1,128,128]{3,2,1,0:T(8,128)} %select_bitcast_fusion), custom_call_target="InvertDiagBlocksLowerTriangular" | custom-call | tf_op jit(solution)/shard_map/jit(cholesky)/cholesky | solution.py:40
  135.8 1.4 constant_dynamic-update-slice_fusion.1
  137.2 2.3 convolution_subtract_fusion
  139.5 48.4 %custom-call.18 = f32[4,128,128]{2,1,0:T(8,128)} custom-call(f32[4,128,128]{2,1,0:T(8,128)} %convolution_subtract_fusion), custom_call_target="Cholesky" | custom-call | tf_op jit(solution)/shard_map/jit(cholesky)/cholesky | solution.py:40
  189.8 2.4 fusion.15
  192.4 5.2 %while.1 = (s32[]{:T(128)}, f32[4,256,256]{2,1,0:T(8,128)S(1)}, s32[2,2]{1,0:T(2,128)S(1)}, f32[2,4,128,128]{3,2,0,1:T(8,128)}, s32[]{:T(128)}) while((s32[]{:T(128)}, f32[4,256,256]{2,1,0:T(8,128)S(1)}, s32[2,2]{1,0:T(2,128)S(1)}, f32[2,4,128,128]{3,2,0,1:T(8,128)}, s32[]{:T(128)}) %tuple.30), condition=%wide.while_cond, body=%wide.while_body.sunk | while | flops 2 | bytes 525421 | solution.py:41
  193.0 2.0 bitcast_dynamic-update-slice_fusion.2
  195.6 2.0 bitcast_dynamic-update-slice_fusion.2
  197.6 79.4 %custom-call.19 = f32[4,2,128,128]{2,3,1,0:T(8,128)S(1)} custom-call(f32[4,2,128,128]{3,2,1,0:T(8,128)} %bitcast.74), custom_call_target="InvertDiagBlocksLowerTriangular" | custom-call | tf_op jit(solution)/shard_map/triangular_solve | solution.py:41
  277.1 14.4 %all_gather.15 = bf16[1,1024,128]{2,1,0:T(8,128)(2,1)S(1)} all-gather(bf16[1,256,128]{2,1,0:T(8,128)(2,1)S(1)} %copy-done.6), channel_id=1, replica_groups=mesh['blk'=8,'col'=4] {'col'}, dimensions={1}, use_global_device_ids=true | all-gather | bytes 327680 | tf_op jit(solution)/shard_map/all_gather | solution.py:24
  291.6 2.0 fusion.7
  293.7 1.6 fusion.12
  295.3 2.4 negate_bitcast_fusion
  298.0 2.7 copy.77
  300.7 9.4 %fusion.4 = bf16[1,4,1024,128]{3,2,1,0:T(8,128)(2,1)} fusion(f32[4,1024,256]{1,0,2:T(4,128)S(1)} %bitcast.68, f32[4,128]{1,0:T(4,128)S(1)} %get-tuple-element.27, f32[4,256,256]{1,2,0:T(8,128)S(1)} %copy-done.3), kind=kOutput, calls=%fused_computation.9 | convolution fusion | flops 1611661312 | bytes 5769216 | tf_op jit(solution)/shard_map/jnc,jmc->jnm/dot_general | solution.py:55
  (64 shorter events, 14.6 us)
Async XLA Ops:
  7.2 286.5 %all-gather.5.cloned.1.call-start = ((), (), s32[]{:S(2)}) async-start(), calls=%async_computation.1 | async-start | bytes 1179648 | tf_op jit(solution)/shard_map/all_gather | solution.py:48
  7.9 287.4 %all-gather.3.cloned.1.call-start = ((), (), s32[]{:S(2)}) async-start(), calls=%async_computation | async-start | bytes 1179648 | tf_op jit(solution)/shard_map/all_gather | solution.py:50
  28.6 3.9 %copy-start.8 = (bf16[128]{0:T(256)(128)(2,1)}, bf16[128]{0:T(256)(128)(2,1)S(1)}, u32[]{:S(2)}) copy-start(bf16[128]{0:T(256)(128)(2,1)S(1)} %compare_convert_fusion) | copy-start | bytes 772
  32.5 1.6 copy-start.4
  44.7 49.6 %copy-start.7 = (pred[128,128]{1,0:T(8,128)(4,1)S(1)}, pred[128,128]{1,0:T(8,128)(4,1)}, u32[]{:S(2)}) copy-start(pred[128,128]{1,0:T(8,128)(4,1)} %iota_compare_fusion.3) | copy-start | bytes 49156
  46.3 1.0 copy-start.2
  94.2 95.7 %copy-start.5 = (pred[256,256]{1,0:T(8,128)(4,1)S(1)}, pred[256,256]{1,0:T(8,128)(4,1)}, u32[]{:S(2)}) copy-start(pred[256,256]{1,0:T(8,128)(4,1)} %iota_compare_fusion.2) | copy-start | bytes 196612
  188.9 1.0 copy-start.1
  192.3 84.8 %copy-start.6 = (bf16[1,256,128]{2,1,0:T(8,128)(2,1)S(1)}, bf16[1,256,128]{2,1,0:T(8,128)(2,1)}, u32[]{:S(2)}) copy-start(bf16[1,256,128]{2,1,0:T(8,128)(2,1)} %param.17) | copy-start | bytes 196612
  192.3 99.2 %copy-start.10 = (s32[1,4]{1,0:T(1,128)S(1)}, s32[1,4]{1,0:T(1,128)}, u32[]{:S(2)}) copy-start(s32[1,4]{1,0:T(1,128)} %param.19) | copy-start | bytes 52
  192.4 101.2 %copy-start.11 = (s32[4]{0:T(128)S(1)}, s32[4]{0:T(128)}, u32[]{:S(2)}) copy-start(s32[4]{0:T(128)} %param.15) | copy-start | bytes 52
  192.4 101.3 %copy-start.9 = (bf16[128]{0:T(256)(128)(2,1)S(1)}, bf16[128]{0:T(256)(128)(2,1)}, u32[]{:S(2)}) copy-start(bf16[128]{0:T(256)(128)(2,1)} %copy-done.8) | copy-start | bytes 772
  295.3 2.4 copy-start
  298.0 2.7 copy-start.3
Sparse Core Ops, SparseCore 0:
  9.9 26.1 all-gather.4
  38.0 23.5 all-gather.2
where the time goes:
time: 318 us; the launch traced here: 317 us
  other arithmetic  228 us (72%)
  blocking collectives  30.3 us (10%)
  local copies, waits for them, and re-layouts  22.5 us (7%)
  matrix products  20 us (6%)
  between operations  14.9 us (5%)
    another operation x10, other arithmetic, on_device(): lower = jnp.linalg.cholesky(gram)  139 us
    another operation x3, other arithmetic, on_device(): lax.linalg.triangular_solve(lower, left.astype(jnp.float32), left_side=Fa...  80.1 us
    all_gather x1, blocking collectives, on_device(): lax.all_gather(row_u, 'col', axis=1, tiled=True)  15.8 us
    all_gather x1, blocking collectives, on_device(): lax.all_gather(row_v, 'col', axis=1, tiled=True)  14.4 us
    dot_general x1, matrix products, on_device(): new_v = jnp.einsum('jnc,jmc->jnm', right, head, precision=HIGH)  9.43 us
  transfers between devices with their start and end apart: 2, of which 0 were waited for; matrix products, arithmetic and copies ran while one was open for 80% of the time, Pallas kernels for 0%

commit v1 on v0

v1 whole, which is shorter than its diff:
```python
import functools
import math

import jax
import jax.numpy as jnp
from jax import lax
from jax.experimental import pallas as pl
from jax.experimental.pallas import tpu as pltpu
from jax.sharding import PartitionSpec as P

HIGH = lax.Precision.HIGHEST
MESH = pl.DeviceIdType.MESH
F32 = jnp.float32
BF16 = jnp.bfloat16
SUB = 8
SUPER = 32


def flip(value, mask):
    bit = 1
    while bit <= mask:
        if mask & bit:
            value = value + bit - 2 * bit * ((value // bit) % 2)
        bit *= 2
    return value


def gather_kernel(
    n_blk, n_col, ru, rv, pu, pv, all_ru, all_rv, all_pu, all_pv,
    own_sem, col_send, col_recv, blk_send, blk_recv, pair_send, pair_recv,
):
    b, c = lax.axis_index("blk"), lax.axis_index("col")
    group, side = b // 2, b % 2
    groups = n_blk // 2
    sibling = group * 2 + 1 - side

    barrier = pltpu.get_barrier_semaphore()
    for step in range(1, n_col):
        pl.semaphore_signal(barrier, inc=1, device_id=(b, (c + step) % n_col), device_id_type=MESH)
    for step in range(1, groups):
        pl.semaphore_signal(
            barrier, inc=1, device_id=(flip(group, step) * 2 + side, c), device_id_type=MESH
        )
    pl.semaphore_signal(barrier, inc=1, device_id=(sibling, c), device_id_type=MESH)
    pl.semaphore_wait(barrier, n_col - 1 + groups - 1 + 1)

    rows = ((ru, all_ru), (rv, all_rv))
    panels = ((pv, all_pv), (pu, all_pu))
    row_copies, blk_copies, pair_copies, own_copies = [], [], [], []
    for at, (source, whole) in enumerate(rows):
        for step in range(1, n_col):
            copy = pltpu.make_async_remote_copy(
                src_ref=source.at[0],
                dst_ref=whole.at[c],
                send_sem=col_send.at[at, step],
                recv_sem=col_recv.at[at, step],
                device_id=(b, (c + step) % n_col),
                device_id_type=MESH,
            )
            copy.start()
            row_copies.append(copy)
    for at, (source, whole) in enumerate(panels):
        for step in range(1, groups):
            copy = pltpu.make_async_remote_copy(
                src_ref=source,
                dst_ref=whole.at[b],
                send_sem=blk_send.at[at, step],
                recv_sem=blk_recv.at[at, step],
                device_id=(flip(group, step) * 2 + side, c),
                device_id_type=MESH,
            )
            copy.start()
            blk_copies.append((at, step, whole, copy))
        copy = pltpu.make_async_remote_copy(
            src_ref=source,
            dst_ref=whole.at[b],
            send_sem=pair_send.at[at, 0],
            recv_sem=pair_recv.at[at, 0],
            device_id=(sibling, c),
            device_id_type=MESH,
        )
        copy.start()
        pair_copies.append(copy)
    for at, (source, target) in enumerate(
        ((ru.at[0], all_ru.at[c]), (rv.at[0], all_rv.at[c]), (pv, all_pv.at[b]), (pu, all_pu.at[b]))
    ):
        copy = pltpu.make_async_copy(source, target, own_sem.at[at])
        copy.start()
        own_copies.append(copy)
    for at, step, whole, copy in blk_copies:
        copy.wait_recv()
        origin = flip(group, step) * 2 + side
        onward = pltpu.make_async_remote_copy(
            src_ref=whole.at[origin],
            dst_ref=whole.at[origin],
            send_sem=pair_send.at[at, step],
            recv_sem=pair_recv.at[at, step],
            device_id=(sibling, c),
            device_id_type=MESH,
        )
        onward.start()
        pair_copies.append(onward)
    for copy in own_copies:
        copy.wait()
    for copy in row_copies:
        copy.wait()
    for _, _, _, copy in blk_copies:
        copy.wait_send()
    for copy in pair_copies:
        copy.wait()


def gather(n_blk, n_col, row_u, row_v, panel_u, panel_v):
    groups = n_blk // 2
    any_space = pl.BlockSpec(memory_space=pl.ANY)
    row_shape = (n_col,) + row_u.shape[1:]
    panel_shape = (n_blk,) + panel_u.shape
    dma = pltpu.SemaphoreType.DMA
    return pl.pallas_call(
        functools.partial(gather_kernel, n_blk, n_col),
        out_shape=[jax.ShapeDtypeStruct(row_shape, BF16)] * 2
        + [jax.ShapeDtypeStruct(panel_shape, BF16)] * 2,
        in_specs=[any_space] * 4,
        out_specs=[any_space] * 4,
        scratch_shapes=[
            dma((4,)),
            dma((2, n_col)),
            dma((2, n_col)),
            dma((2, groups)),
            dma((2, groups)),
            dma((2, groups)),
            dma((2, groups)),
        ],
        compiler_params=pltpu.CompilerParams(collective_id=0, has_side_effects=True),
        name="gather",
    )(row_u, row_v, panel_u, panel_v)


def across(first, second, precision=None):
    return lax.dot_general(
        first, second, (((0,), (0,)), ((), ())), precision=precision, preferred_element_type=F32
    )


def split(value):
    high = value.astype(BF16)
    return high, (value - high.astype(F32)).astype(BF16)


def eliminate(work, width, tiles):
    lane = lax.broadcasted_iota(jnp.int32, (SUB, width), 1)

    def spread(row, at):
        return jnp.broadcast_to(row[:, at : at + 1], (SUB, width))

    for top in range(0, width, SUPER):
        for base in range(top, top + SUPER, SUB):
            within = (lane >= base) & (lane < base + SUB)
            rows = [work[pl.ds((base + i) * SUB, SUB), :] for i in range(SUB)]
            entry = {
                (i, j): spread(rows[i], base + j) for i in range(SUB) for j in range(i, SUB)
            }
            rows = [
                jnp.where(within, (lane == base + i).astype(F32), rows[i]) for i in range(SUB)
            ]
            for k in range(SUB):
                inverse = lax.rsqrt(entry[k, k])
                rows[k] = rows[k] * inverse
                factor = {j: entry[k, j] * inverse for j in range(k + 1, SUB)}
                for i in range(k + 1, SUB):
                    for j in range(i, SUB):
                        entry[i, j] = entry[i, j] - factor[i] * factor[j]
                for i in range(k + 1, SUB):
                    rows[i] = rows[i] - factor[i] * rows[k]
            for i in range(SUB):
                work[pl.ds((base + i) * SUB, SUB), :] = rows[i]
            for i in range(base + SUB, top + SUPER):
                row = jnp.where(within, 0.0, work[pl.ds(i * SUB, SUB), :])
                for k in range(SUB):
                    row = row - spread(rows[k], i) * rows[k]
                work[pl.ds(i * SUB, SUB), :] = row
        below = top + SUPER
        if below < width:
            rest = width - below
            column = lax.broadcasted_iota(jnp.int32, (rest, width), 1)
            done = (column >= top) & (column < below)
            pivot = lax.broadcasted_iota(jnp.int32, (SUPER, width), 0) + top
            ahead = lax.broadcasted_iota(jnp.int32, (SUPER, width), 1)
            ahead = (ahead > pivot) & (ahead < below)
            for t in range(tiles):
                pivots = work[pl.ds(top * SUB + t, SUPER, stride=SUB), :]
                update = across(pivots, jnp.where(ahead, 0.0, pivots), HIGH)[below:, :]
                old = work[pl.ds(below * SUB + t, rest, stride=SUB), :]
                work[pl.ds(below * SUB + t, rest, stride=SUB), :] = (
                    jnp.where(done, 0.0, old) - update
                )


def tile_kernel(
    tile_rank, band_rank, row_rank, target_rank,
    tile_u, tile_v, all_ru, all_rv, all_pu, all_pv, new_u, new_v,
    work, left, gram_t, gram_r,
):
    tiles, order, width = tile_u.shape[1:]
    half = width // 2
    scale = math.sqrt(order)
    row = lax.broadcasted_iota(jnp.int32, (width, width), 0)
    col = lax.broadcasted_iota(jnp.int32, (width, width), 1)
    place = col // 2
    even = col % 2 == 0
    ru = all_ru[...]
    rv = all_rv[...]
    rr = row_rank[0]
    for t in range(tiles):
        tr = tile_rank[0, t]
        tu = tile_u[0, t]
        pick_t = ((row == place) & even & (row < tr)).astype(BF16)
        pick_r = ((row == place) & jnp.logical_not(even) & (row < rr)).astype(BF16)
        both = jnp.concatenate([tu, ru], axis=1)
        first = jnp.dot(
            both, jnp.concatenate([pick_t, pick_r], axis=0), preferred_element_type=F32
        ).astype(BF16)
        left[t] = first
        gram_t[t] = across(tu, first)
        gram_r[t] = across(ru, first)
        spare = (row == col) & (place >= jnp.where(even, tr, rr))
        work[pl.ds(t, width, stride=SUB), :] = across(first, first) + spare.astype(F32)
    eliminate(work, width, tiles)
    for t in range(tiles):
        keep = col < target_rank[0, t]
        inverse = jnp.where(col <= row, work[pl.ds(t, width, stride=SUB), :], 0.0).T
        inverse = jnp.where(keep, inverse, 0.0)
        high, low = split(inverse * scale)
        first = left[t]
        new_u[0, t] = jnp.dot(
            jnp.concatenate([first, first], axis=1),
            jnp.concatenate([high, low], axis=0),
            preferred_element_type=F32,
        ).astype(BF16)
        pv = all_pv[:, t].reshape(order, width)
        pu = all_pu[:, t].reshape(order, width)
        core = jnp.where(row < rr, across(rv, pv), 0.0)
        head_t = jnp.dot(gram_t[t], inverse, precision=HIGH, preferred_element_type=F32)
        head_r = jnp.dot(gram_r[t], inverse, precision=HIGH, preferred_element_type=F32)
        panel = across(core, head_r, HIGH)
        head_t = jnp.where(row < tile_rank[0, t], head_t, 0.0) / scale
        panel = jnp.where(row < band_rank[t], -panel, 0.0) / scale
        high, low = split(jnp.concatenate([head_t, panel], axis=0))
        right = jnp.concatenate([tile_v[0, t], pu], axis=1)
        new_v[0, t] = (
            jnp.dot(right, high, preferred_element_type=F32)
            + jnp.dot(right, low, preferred_element_type=F32)
        ).astype(BF16)


def update(tile_u, tile_v, tile_rank, all_pu, all_pv, band_rank, all_ru, all_rv, row_rank, target_rank):
    tiles, order, width = tile_u.shape[1:]
    smem = pl.BlockSpec(memory_space=pltpu.SMEM)
    vmem = pl.BlockSpec(memory_space=pltpu.VMEM)
    return pl.pallas_call(
        tile_kernel,
        out_shape=[jax.ShapeDtypeStruct(tile_u.shape, BF16)] * 2,
        in_specs=[smem] * 4 + [vmem] * 6,
        out_specs=[vmem] * 2,
        scratch_shapes=[
            pltpu.VMEM((width * SUB, width), F32),
            pltpu.VMEM((tiles, order, width), BF16),
            pltpu.VMEM((tiles, width, width), F32),
            pltpu.VMEM((tiles, width, width), F32),
        ],
        compiler_params=pltpu.CompilerParams(vmem_limit_bytes=48 * 1024 * 1024),
        name="tiles",
    )(tile_rank, band_rank, row_rank, target_rank, tile_u, tile_v, all_ru, all_rv, all_pu, all_pv)


def on_device(
    n_blk, n_col,
    tile_u, tile_v, tile_rank, panel_u, panel_v, band_rank, row_u, row_v, row_rank, target_rank,
):
    order, width = tile_u.shape[2:]
    all_ru, all_rv, all_pu, all_pv = gather(n_blk, n_col, row_u, row_v, panel_u, panel_v)
    all_ru, all_rv = all_ru.reshape(order, width), all_rv.reshape(order, width)
    if panel_u.shape[1] % 16:
        all_pu, all_pv = (
            jnp.swapaxes(each, 0, 1).reshape(1, each.shape[1], order, width)
            for each in (all_pu, all_pv)
        )
    return tuple(
        update(
            tile_u, tile_v, tile_rank, all_pu, all_pv, band_rank, all_ru, all_rv, row_rank,
            target_rank,
        )
    )


def solution(mesh):
    return jax.shard_map(
        functools.partial(on_device, mesh.shape["blk"], mesh.shape["col"]),
        mesh=mesh,
        in_specs=(
            P("blk", "col", None, None),
            P("blk", "col", None, None),
            P("blk", "col"),
            P("col", "blk", None),
            P("col", "blk", None),
            P("col"),
            P("blk", "col", None),
            P("blk", "col", None),
            P("blk"),
            P("blk", "col"),
        ),
        out_specs=(P("blk", "col", None, None), P("blk", "col", None, None)),
        check_vma=False,
    )
```

time: 318 us -> 44.1 us (0.14)
  other arithmetic: 228 us -> 0 us
  Pallas kernels: 0 us -> 35 us
  blocking collectives: 30.3 us -> 0 us
  matrix products: 20 us -> 0 us
  local copies, waits for them, and re-layouts: 22.5 us -> 7.46 us
  between operations: 14.9 us -> 1.32 us
    another operation x15 -> x0, other arithmetic: 219 us -> none  [the longest x10 139 us: on_device(): lower = jnp.linalg.cholesky(gram)]
    pallas_call x0 -> x2, Pallas kernels: none -> 35 us  [the longest x1 21.3 us: gather(): pl.pallas_call(functools.partial(gather_kernel, n_blk, n_col), out_shape=...]
    all_gather x2 -> x0, blocking collectives: 30.3 us -> none  [the longest x1 15.8 us: on_device(): lax.all_gather(row_u, 'col', axis=1, tiled=True)]
    dot_general x4 -> x0, matrix products: 14.2 us -> none  [the longest x1 9.43 us: on_device(): new_v = jnp.einsum('jnc,jmc->jnm', right, head, precision=HIGH)]
    another operation x13 -> x0, local copies, waits for them, and re-layouts: 11.2 us -> none  [the longest x4 5.76 us: pair_columns(): joined = jnp.stack([first, second], axis=-1)]
    another operation x3 -> x0, matrix products: 5.75 us -> none  [the longest x2 3.74 us: on_device(): lower = jnp.linalg.cholesky(gram)]
    convert_element_type x7 -> x0, other arithmetic: 3.88 us -> none  [the longest x1 1.62 us: on_device(): right_tile = (tile_v[0] * tile_keep[:, None, :]).astype(jnp.float32)]
    unnamed x26 -> x18, local copies, waits for them, and re-layouts: 4.7 us -> 7.46 us
  transfers between devices with their start and end apart: 2 -> 0, of which waited for: 0 -> 0; matrix products, arithmetic and copies ran while one was open for 80% -> 0% of each run, Pallas kernels for 0% -> 0%
where the time goes in v1:
time: 44.1 us; the launch traced here: 43.7 us
  Pallas kernels  35 us (79%)
  local copies, waits for them, and re-layouts  7.46 us (17%)
  between operations  1.32 us (3%)
    pallas_call x1, Pallas kernels, gather(): pl.pallas_call(functools.partial(gather_kernel, n_blk, n_col), out_shape=...  21.3 us
    pallas_call x1, Pallas kernels, update(): pl.pallas_call(tile_kernel, out_shape=[jax.ShapeDtypeStruct(tile_u.shape,...  13.7 us
    unnamed x18, local copies, waits for them, and re-layouts  7.46 us

profile of v1, /device:TPU:0, one launch (start us, length us, event | category | flops | bytes accessed | tf_op | source)
XLA Modules:
  0.0 43.7 jit_solution(6682294564498673952)
XLA Ops:
  1.3 21.3 %gather.1 = (bf16[4,256,128]{2,1,0:T(8,128)(2,1)}, bf16[4,256,128]{2,1,0:T(8,128)(2,1)}, bf16[8,4,128,128]{3,2,1,0:T(8,128)(2,1)}, bf16[8,4,128,128]{3,2,1,0:T(8,128)(2,1)}) custom-call(bf16[1,256,128]{2,1,0:T(8,128)(2,1)} %ru.1, bf16[1,256,128]{2,1,0:T(8,128)(2,1)} %rv.1, bf16[4,128,128]{2,1,0:T(8,128)(2,1)} %pu.1, bf16[4,128,128]{2,1,0:T(8,128)(2,1)} %pv.1), custom_call_target="tpu_custom_call" | custom-call | tf_op jit(solution)/shard_map/gather/pallas_call | solution.py:119
  22.6 0.0 copy-start.6
  22.6 0.0 copy-start.7
  22.6 0.0 copy-start.8
  22.6 0.6 %copy-done.6 = s32[1,4]{1,0:T(1,128)S(1)} copy-done((s32[1,4]{1,0:T(1,128)S(1)}, s32[1,4]{1,0:T(1,128)}, u32[]{:S(2)}) %copy-start.6) | copy-done | bytes 40
  23.2 0.0 copy-done.7
  23.2 0.0 copy-done.8
  23.3 0.0 copy-start
  23.3 1.2 %copy-done = bf16[1,4,1024,128]{3,2,1,0:T(8,128)(2,1)S(1)} copy-done((bf16[1,4,1024,128]{3,2,1,0:T(8,128)(2,1)S(1)}, bf16[1,4,1024,128]{3,2,1,0:T(8,128)(2,1)}, u32[]{:S(2)}) %copy-start) | copy-done | bytes 1048600
  24.5 0.0 copy-start.1
  24.5 1.2 %copy-done.1 = bf16[1,4,1024,128]{3,2,1,0:T(8,128)(2,1)S(1)} copy-done((bf16[1,4,1024,128]{3,2,1,0:T(8,128)(2,1)S(1)}, bf16[1,4,1024,128]{3,2,1,0:T(8,128)(2,1)}, u32[]{:S(2)}) %copy-start.1) | copy-done | bytes 1048600
  25.7 0.0 copy-start.2
  25.7 1.2 %copy-done.2 = bf16[8,4,128,128]{3,2,1,0:T(8,128)(2,1)S(1)} copy-done((bf16[8,4,128,128]{3,2,1,0:T(8,128)(2,1)S(1)}, bf16[8,4,128,128]{3,2,1,0:T(8,128)(2,1)}, u32[]{:S(2)}) %copy-start.2) | copy-done | bytes 1048600
  26.9 0.0 copy-start.3
  26.9 1.2 %copy-done.3 = bf16[8,4,128,128]{3,2,1,0:T(8,128)(2,1)S(1)} copy-done((bf16[8,4,128,128]{3,2,1,0:T(8,128)(2,1)S(1)}, bf16[8,4,128,128]{3,2,1,0:T(8,128)(2,1)}, u32[]{:S(2)}) %copy-start.3) | copy-done | bytes 1048600
  28.2 0.0 copy-start.4
  28.2 0.9 %copy-done.4 = bf16[4,256,128]{2,1,0:T(8,128)(2,1)S(1)} copy-done((bf16[4,256,128]{2,1,0:T(8,128)(2,1)S(1)}, bf16[4,256,128]{2,1,0:T(8,128)(2,1)}, u32[]{:S(2)}) %copy-start.4) | copy-done | bytes 262168
  29.1 0.0 copy-start.5
  29.1 0.9 %copy-done.5 = bf16[4,256,128]{2,1,0:T(8,128)(2,1)S(1)} copy-done((bf16[4,256,128]{2,1,0:T(8,128)(2,1)S(1)}, bf16[4,256,128]{2,1,0:T(8,128)(2,1)}, u32[]{:S(2)}) %copy-start.5) | copy-done | bytes 262168
  30.1 13.7 %tiles.1 = (bf16[1,4,1024,128]{3,2,1,0:T(8,128)(2,1)}, bf16[1,4,1024,128]{3,2,1,0:T(8,128)(2,1)}) custom-call(s32[1,4]{1,0:T(1,128)S(1)} %copy-done.6, s32[4]{0:T(128)S(1)} %copy-done.7, s32[1]{0:T(128)S(6)} %copy.12.row_rank, s32[1,4]{1,0:T(1,128)S(1)} %copy-done.8, bf16[1,4,1024,128]{3,2,1,0:T(8,128)(2,1)S(1)} %copy-done, ...), custom_call_target="tpu_custom_call" | custom-call | tf_op jit(solution)/shard_map/tiles/pallas_call | solution.py:260
Async XLA Ops:
  22.6 0.7 %copy-start.6 = (s32[1,4]{1,0:T(1,128)S(1)}, s32[1,4]{1,0:T(1,128)}, u32[]{:S(2)}) copy-start(s32[1,4]{1,0:T(1,128)} %tile_rank.1) | copy-start | bytes 52
  22.6 0.7 %copy-start.7 = (s32[4]{0:T(128)S(1)}, s32[4]{0:T(128)}, u32[]{:S(2)}) copy-start(s32[4]{0:T(128)} %band_rank.1) | copy-start | bytes 52
  22.6 0.7 %copy-start.8 = (s32[1,4]{1,0:T(1,128)S(1)}, s32[1,4]{1,0:T(1,128)}, u32[]{:S(2)}) copy-start(s32[1,4]{1,0:T(1,128)} %target_rank.1) | copy-start | bytes 52
  23.3 1.2 %copy-start = (bf16[1,4,1024,128]{3,2,1,0:T(8,128)(2,1)S(1)}, bf16[1,4,1024,128]{3,2,1,0:T(8,128)(2,1)}, u32[]{:S(2)}) copy-start(bf16[1,4,1024,128]{3,2,1,0:T(8,128)(2,1)} %tile_u.1) | copy-start | bytes 3145732
  24.5 1.2 %copy-start.1 = (bf16[1,4,1024,128]{3,2,1,0:T(8,128)(2,1)S(1)}, bf16[1,4,1024,128]{3,2,1,0:T(8,128)(2,1)}, u32[]{:S(2)}) copy-start(bf16[1,4,1024,128]{3,2,1,0:T(8,128)(2,1)} %tile_v.1) | copy-start | bytes 3145732
  25.7 1.2 %copy-start.2 = (bf16[8,4,128,128]{3,2,1,0:T(8,128)(2,1)S(1)}, bf16[8,4,128,128]{3,2,1,0:T(8,128)(2,1)}, u32[]{:S(2)}) copy-start(bf16[8,4,128,128]{3,2,1,0:T(8,128)(2,1)} %get-tuple-element.8.all_pu) | copy-start | bytes 3145732
  26.9 1.2 %copy-start.3 = (bf16[8,4,128,128]{3,2,1,0:T(8,128)(2,1)S(1)}, bf16[8,4,128,128]{3,2,1,0:T(8,128)(2,1)}, u32[]{:S(2)}) copy-start(bf16[8,4,128,128]{3,2,1,0:T(8,128)(2,1)} %get-tuple-element.9.all_pv) | copy-start | bytes 3145732
  28.2 0.9 %copy-start.4 = (bf16[4,256,128]{2,1,0:T(8,128)(2,1)S(1)}, bf16[4,256,128]{2,1,0:T(8,128)(2,1)}, u32[]{:S(2)}) copy-start(bf16[4,256,128]{2,1,0:T(8,128)(2,1)} %get-tuple-element.6) | copy-start | bytes 786436
  29.1 0.9 %copy-start.5 = (bf16[4,256,128]{2,1,0:T(8,128)(2,1)S(1)}, bf16[4,256,128]{2,1,0:T(8,128)(2,1)}, u32[]{:S(2)}) copy-start(bf16[4,256,128]{2,1,0:T(8,128)(2,1)} %get-tuple-element.7) | copy-start | bytes 786436

commit v2 on v1

--- a/solution.py
+++ b/solution.py
@@ -142,18 +142,54 @@
     )
 
 
+def first_half(t, tu, ru, tr, rr, left, gram_t, gram_r, work):
+    width = tu.shape[1]
+    row = lax.broadcasted_iota(jnp.int32, (width, width), 0)
+    col = lax.broadcasted_iota(jnp.int32, (width, width), 1)
+    place = col // 2
+    even = col % 2 == 0
+    pick_t = ((row == place) & even & (row < tr)).astype(BF16)
+    pick_r = ((row == place) & jnp.logical_not(even) & (row < rr)).astype(BF16)
+    both = jnp.concatenate([tu, ru], axis=1)
+    first = jnp.dot(
+        both, jnp.concatenate([pick_t, pick_r], axis=0), preferred_element_type=F32
+    ).astype(BF16)
+    left[t] = first
+    gram_t[t] = across(tu, first)
+    gram_r[t] = across(ru, first)
+    spare = (row == col) & (place >= jnp.where(even, tr, rr))
+    work[pl.ds(t, width, stride=SUB), :] = across(first, first) + spare.astype(F32)
+
+
+def factors(t, scale, ranks, core, gram_t, gram_r, work):
+    tr, br, tk = ranks
+    width = core.shape[0]
+    row = lax.broadcasted_iota(jnp.int32, (width, width), 0)
+    col = lax.broadcasted_iota(jnp.int32, (width, width), 1)
+    inverse = jnp.where(col <= row, work[pl.ds(t, width, stride=SUB), :], 0.0).T
+    inverse = jnp.where(col < tk, inverse, 0.0)
+    head_t = jnp.dot(gram_t[t], inverse, precision=HIGH, preferred_element_type=F32)
+    head_r = jnp.dot(gram_r[t], inverse, precision=HIGH, preferred_element_type=F32)
+    panel = across(core, head_r, HIGH)
+    head_t = jnp.where(row < tr, head_t, 0.0) / scale
+    panel = jnp.where(row < br, -panel, 0.0) / scale
+    return split(inverse * scale), split(jnp.concatenate([head_t, panel], axis=0))
+
+
 def split(value):
     high = value.astype(BF16)
     return high, (value - high.astype(F32)).astype(BF16)
 
 
-def eliminate(work, width, tiles):
+def eliminate(work, width, tiles, between={}):
     lane = lax.broadcasted_iota(jnp.int32, (SUB, width), 1)
 
     def spread(row, at):
         return jnp.broadcast_to(row[:, at : at + 1], (SUB, width))
 
     for top in range(0, width, SUPER):
+        if top in between:
+            between[top]()
         for base in range(top, top + SUPER, SUB):
             within = (lane >= base) & (lane < base + SUB)
             rows = [work[pl.ds((base + i) * SUB, SUB), :] for i in range(SUB)]
@@ -196,61 +232,242 @@
                 )
 
 
+def products(first, u_parts, tv, pu, v_parts):
+    new_u = jnp.dot(
+        jnp.concatenate([first, first], axis=1), u_parts, preferred_element_type=F32
+    ).astype(BF16)
+    right = jnp.concatenate([tv, pu], axis=1)
+    new_v = (
+        jnp.dot(right, v_parts[0], preferred_element_type=F32)
+        + jnp.dot(right, v_parts[1], preferred_element_type=F32)
+    ).astype(BF16)
+    return new_u, new_v
+
+
 def tile_kernel(
     tile_rank, band_rank, row_rank, target_rank,
     tile_u, tile_v, all_ru, all_rv, all_pu, all_pv, new_u, new_v,
     work, left, gram_t, gram_r,
 ):
     tiles, order, width = tile_u.shape[1:]
-    half = width // 2
-    scale = math.sqrt(order)
-    row = lax.broadcasted_iota(jnp.int32, (width, width), 0)
-    col = lax.broadcasted_iota(jnp.int32, (width, width), 1)
-    place = col // 2
-    even = col % 2 == 0
     ru = all_ru[...]
     rv = all_rv[...]
     rr = row_rank[0]
+    row = lax.broadcasted_iota(jnp.int32, (width, width), 0)
     for t in range(tiles):
-        tr = tile_rank[0, t]
-        tu = tile_u[0, t]
-        pick_t = ((row == place) & even & (row < tr)).astype(BF16)
-        pick_r = ((row == place) & jnp.logical_not(even) & (row < rr)).astype(BF16)
-        both = jnp.concatenate([tu, ru], axis=1)
-        first = jnp.dot(
-            both, jnp.concatenate([pick_t, pick_r], axis=0), preferred_element_type=F32
-        ).astype(BF16)
-        left[t] = first
-        gram_t[t] = across(tu, first)
-        gram_r[t] = across(ru, first)
-        spare = (row == col) & (place >= jnp.where(even, tr, rr))
-        work[pl.ds(t, width, stride=SUB), :] = across(first, first) + spare.astype(F32)
+        first_half(t, tile_u[0, t], ru, tile_rank[0, t], rr, left, gram_t, gram_r, work)
     eliminate(work, width, tiles)
     for t in range(tiles):
-        keep = col < target_rank[0, t]
-        inverse = jnp.where(col <= row, work[pl.ds(t, width, stride=SUB), :], 0.0).T
-        inverse = jnp.where(keep, inverse, 0.0)
-        high, low = split(inverse * scale)
-        first = left[t]
-        new_u[0, t] = jnp.dot(
-            jnp.concatenate([first, first], axis=1),
-            jnp.concatenate([high, low], axis=0),
-            preferred_element_type=F32,
-        ).astype(BF16)
-        pv = all_pv[:, t].reshape(order, width)
-        pu = all_pu[:, t].reshape(order, width)
-        core = jnp.where(row < rr, across(rv, pv), 0.0)
-        head_t = jnp.dot(gram_t[t], inverse, precision=HIGH, preferred_element_type=F32)
-        head_r = jnp.dot(gram_r[t], inverse, precision=HIGH, preferred_element_type=F32)
-        panel = across(core, head_r, HIGH)
-        head_t = jnp.where(row < tile_rank[0, t], head_t, 0.0) / scale
-        panel = jnp.where(row < band_rank[t], -panel, 0.0) / scale
-        high, low = split(jnp.concatenate([head_t, panel], axis=0))
-        right = jnp.concatenate([tile_v[0, t], pu], axis=1)
-        new_v[0, t] = (
-            jnp.dot(right, high, preferred_element_type=F32)
-            + jnp.dot(right, low, preferred_element_type=F32)
-        ).astype(BF16)
+        core = jnp.where(row < rr, across(rv, all_pv[:, t].reshape(order, width)), 0.0)
+        ranks = (tile_rank[0, t], band_rank[t], target_rank[0, t])
+        u_parts, v_parts = factors(t, math.sqrt(order), ranks, core, gram_t, gram_r, work)
+        new_u[0, t], new_v[0, t] = products(
+            left[t], jnp.concatenate(u_parts, axis=0), tile_v[0, t],
+            all_pu[:, t].reshape(order, width), v_parts,
+        )
+
+
+def factor_kernel(
+    n_blk, n_col, tile_rank, band_rank, row_rank, target_rank, tile_u, ru, rv, pu, pv,
+    all_pu, left_out, u_out, v_out,
+    tu, all_ru, all_rv, all_pv, left, work, gram_t, gram_r, cores,
+    own_sem, tile_sem, left_sem, col_send, col_recv, blk_send, blk_recv, pair_send, pair_recv,
+):
+    tiles, order, width = tu.shape
+    b, c = lax.axis_index("blk"), lax.axis_index("col")
+    group, side = b // 2, b % 2
+    sibling = group * 2 + 1 - side
+    near = {step: flip(group, step) * 2 + side for step in (1, 2, 3)}
+
+    locals_ = [
+        pltpu.make_async_copy(ru.at[0], all_ru.at[c], own_sem.at[0]),
+        pltpu.make_async_copy(rv.at[0], all_rv.at[c], own_sem.at[1]),
+        pltpu.make_async_copy(pv, all_pv.at[b], own_sem.at[2]),
+        pltpu.make_async_copy(pu, all_pu.at[b], own_sem.at[3]),
+    ]
+    tile_copies = [
+        pltpu.make_async_copy(tile_u.at[0, t], tu.at[t], tile_sem.at[t]) for t in range(tiles)
+    ]
+    for copy in locals_ + tile_copies:
+        copy.start()
+
+    barrier = pltpu.get_barrier_semaphore()
+    peers = [(b, (c + step) % n_col) for step in range(1, n_col)]
+    peers += [(near[1], c), (near[2], c), (sibling, c)]
+    for peer in peers:
+        pl.semaphore_signal(barrier, inc=1, device_id=peer, device_id_type=MESH)
+    pl.semaphore_wait(barrier, len(peers))
+
+    def row_sends(at, source, whole):
+        copies = [
+            pltpu.make_async_remote_copy(
+                src_ref=source.at[0],
+                dst_ref=whole.at[c],
+                send_sem=col_send.at[at, step],
+                recv_sem=col_recv.at[at, step],
+                device_id=(b, (c + step) % n_col),
+                device_id_type=MESH,
+            )
+            for step in range(1, n_col)
+        ]
+        for copy in copies:
+            copy.start()
+        return copies
+
+    def panel_send(at, step, source, whole, slot, target, send, recv):
+        copy = pltpu.make_async_remote_copy(
+            src_ref=source,
+            dst_ref=whole.at[slot],
+            send_sem=send.at[at, step],
+            recv_sem=recv.at[at, step],
+            device_id=(target, c),
+            device_id_type=MESH,
+        )
+        copy.start()
+        return copy
+
+    ru_copies = row_sends(0, ru, all_ru)
+    wholes = (all_pv, all_pu)
+    blk_copies, pair_copies = {}, []
+    for at, source in enumerate((pv, pu)):
+        for step in (1, 2):
+            blk_copies[at, step] = panel_send(
+                at, step, source, wholes[at], b, near[step], blk_send, blk_recv
+            )
+    for at, source in enumerate((pv, pu)):
+        pair_copies.append(
+            panel_send(at, 0, source, wholes[at], b, sibling, pair_send, pair_recv)
+        )
+
+    def pass_on(at, step):
+        blk_copies[at, step].wait_recv()
+        slot = near[step]
+        here = wholes[at].at[slot]
+        if (at, step) == (0, 2):
+            blk_copies[0, 3] = panel_send(0, 3, here, all_pv, slot, near[1], blk_send, blk_recv)
+        if (at, step) == (1, 1):
+            blk_copies[1, 3] = panel_send(1, 3, here, all_pu, slot, near[2], blk_send, blk_recv)
+        pair_copies.append(
+            panel_send(at, step, here, wholes[at], slot, sibling, pair_send, pair_recv)
+        )
+
+    locals_[0].wait()
+    for copy in ru_copies:
+        copy.wait_recv()
+    rv_copies = row_sends(1, rv, all_rv)
+    ru_all = all_ru[...].reshape(order, width)
+    rr = row_rank[0]
+    left_copies = []
+    for t in range(tiles):
+        tile_copies[t].wait()
+        first_half(t, tu[t], ru_all, tile_rank[0, t], rr, left, gram_t, gram_r, work)
+        if t == tiles // 2 - 1:
+            for at, step in ((0, 2), (1, 1), (0, 1), (1, 2)):
+                pass_on(at, step)
+    for t in range(tiles):
+        copy = pltpu.make_async_copy(left.at[t], left_out.at[t], left_sem.at[t])
+        copy.start()
+        left_copies.append(copy)
+
+    def diagonal():
+        pass_on(0, 3)
+        pass_on(1, 3)
+
+    def cores_ready():
+        row = lax.broadcasted_iota(jnp.int32, (width, width), 0)
+        for copy in locals_[1:]:
+            copy.wait()
+        for copy in rv_copies + pair_copies:
+            copy.wait_recv()
+        rv_all = all_rv[...].reshape(order, width)
+        for t in range(tiles):
+            cores[t] = jnp.where(
+                row < rr, across(rv_all, all_pv[:, t].reshape(order, width)), 0.0
+            )
+
+    eliminate(work, width, tiles, {SUPER: diagonal, 3 * SUPER: cores_ready})
+    for t in range(tiles):
+        ranks = (tile_rank[0, t], band_rank[t], target_rank[0, t])
+        u_parts, v_parts = factors(t, math.sqrt(order), ranks, cores[t], gram_t, gram_r, work)
+        u_out[t] = jnp.concatenate(u_parts, axis=0)
+        v_out[t, 0], v_out[t, 1] = v_parts
+    for copy in left_copies:
+        copy.wait()
+    for copy in ru_copies + rv_copies + list(blk_copies.values()) + pair_copies:
+        copy.wait_send()
+
+
+def factor(n_blk, n_col, tile_u, tile_rank, panel_u, panel_v, band_rank, row_u, row_v, row_rank, target_rank):
+    tiles, order, width = tile_u.shape[1:]
+    smem = pl.BlockSpec(memory_space=pltpu.SMEM)
+    vmem = pl.BlockSpec(memory_space=pltpu.VMEM)
+    any_space = pl.BlockSpec(memory_space=pl.ANY)
+    dma = pltpu.SemaphoreType.DMA
+    row_shape = (n_col,) + row_u.shape[1:]
+    panel_shape = (n_blk,) + panel_u.shape
+    return pl.pallas_call(
+        functools.partial(factor_kernel, n_blk, n_col),
+        out_shape=[
+            jax.ShapeDtypeStruct(panel_shape, BF16),
+            jax.ShapeDtypeStruct((tiles, order, width), BF16),
+            jax.ShapeDtypeStruct((tiles, 2 * width, width), BF16),
+            jax.ShapeDtypeStruct((tiles, 2, 2 * width, width), BF16),
+        ],
+        in_specs=[smem] * 4 + [any_space] * 5,
+        out_specs=[any_space] * 2 + [vmem] * 2,
+        scratch_shapes=[
+            pltpu.VMEM((tiles, order, width), BF16),
+            pltpu.VMEM(row_shape, BF16),
+            pltpu.VMEM(row_shape, BF16),
+            pltpu.VMEM(panel_shape, BF16),
+            pltpu.VMEM((tiles, order, width), BF16),
+            pltpu.VMEM((width * SUB, width), F32),
+            pltpu.VMEM((tiles, width, width), F32),
+            pltpu.VMEM((tiles, width, width), F32),
+            pltpu.VMEM((tiles, width, width), F32),
+            dma((4,)),
+            dma((tiles,)),
+            dma((tiles,)),
+            dma((2, n_col)),
+            dma((2, n_col)),
+            dma((2, 4)),
+            dma((2, 4)),
+            dma((2, 4)),
+            dma((2, 4)),
+        ],
+        compiler_params=pltpu.CompilerParams(
+            collective_id=0, has_side_effects=True, vmem_limit_bytes=32 * 1024 * 1024
+        ),
+        name="factor",
+    )(tile_rank, band_rank, row_rank, target_rank, tile_u, row_u, row_v, panel_u, panel_v)
+
+
+def product_kernel(left, u_parts, tile_v, all_pu, v_parts, new_u, new_v):
+    order, width = left.shape[1:]
+    new_u[0, 0], new_v[0, 0] = products(
+        left[0], u_parts[0], tile_v[0, 0], all_pu[:, 0].reshape(order, width), v_parts[0]
+    )
+
+
+def product(left, u_parts, tile_v, all_pu, v_parts):
+    tiles, order, width = left.shape
+    tile = pl.BlockSpec((1, 1, order, width), lambda t: (0, t, 0, 0))
+    n_blk, _, rows, _ = all_pu.shape
+    return pl.pallas_call(
+        product_kernel,
+        grid=(tiles,),
+        out_shape=[jax.ShapeDtypeStruct(tile_v.shape, BF16)] * 2,
+        in_specs=[
+            pl.BlockSpec((1, order, width), lambda t: (t, 0, 0)),
+            pl.BlockSpec((1, 2 * width, width), lambda t: (t, 0, 0)),
+            tile,
+            pl.BlockSpec((n_blk, 1, rows, width), lambda t: (0, t, 0, 0)),
+            pl.BlockSpec((1, 2, 2 * width, width), lambda t: (t, 0, 0, 0)),
+        ],
+        out_specs=[tile] * 2,
+        compiler_params=pltpu.CompilerParams(vmem_limit_bytes=32 * 1024 * 1024),
+        name="product",
+    )(left, u_parts, tile_v, all_pu, v_parts)
 
 
 def update(tile_u, tile_v, tile_rank, all_pu, all_pv, band_rank, all_ru, all_rv, row_rank, target_rank):
@@ -278,6 +495,12 @@
     tile_u, tile_v, tile_rank, panel_u, panel_v, band_rank, row_u, row_v, row_rank, target_rank,
 ):
     order, width = tile_u.shape[2:]
+    if n_blk == 8 and panel_u.shape[1] % 16 == 0:
+        all_pu, left, u_parts, v_parts = factor(
+            n_blk, n_col, tile_u, tile_rank, panel_u, panel_v, band_rank, row_u, row_v, row_rank,
+            target_rank,
+        )
+        return tuple(product(left, u_parts, tile_v, all_pu, v_parts))
     all_ru, all_rv, all_pu, all_pv = gather(n_blk, n_col, row_u, row_v, panel_u, panel_v)
     all_ru, all_rv = all_ru.reshape(order, width), all_rv.reshape(order, width)
     if panel_u.shape[1] % 16:

time: 44.1 us -> 34.1 us (0.77)
  Pallas kernels: 35 us -> 27.7 us
  local copies, waits for them, and re-layouts: 7.46 us -> 4.72 us
    pallas_call x2, Pallas kernels: 35 us -> 27.7 us  [the longest x1 24.5 us: factor(): pl.pallas_call(functools.partial(factor_kernel, n_blk, n_col), out_shape=...]
    unnamed x18, local copies, waits for them, and re-layouts: 7.46 us -> 4.72 us
where the time goes in v2:
time: 34.1 us; the launch traced here: 33.8 us
  Pallas kernels  27.7 us (81%)
  local copies, waits for them, and re-layouts  4.72 us (14%)
  between operations  1.38 us (4%)
    pallas_call x1, Pallas kernels, factor(): pl.pallas_call(functools.partial(factor_kernel, n_blk, n_col), out_shape=...  24.5 us
    unnamed x18, local copies, waits for them, and re-layouts  4.72 us
    pallas_call x1, Pallas kernels, product(): pl.pallas_call(product_kernel, grid=(tiles,), out_shape=[jax.ShapeDtypeSt...  3.25 us

profile of v2, /device:TPU:0, one launch (start us, length us, event | category | flops | bytes accessed | tf_op | source)
XLA Modules:
  0.0 33.8 jit_solution(174292831774239226)
XLA Ops:
  0.6 0.0 copy-start.8
  0.6 0.0 copy-start.7
  0.7 0.0 copy-start.6
  1.3 0.0 copy-done.8
  1.3 0.0 copy-done.7
  1.4 0.0 copy-done.6
  1.4 0.0 copy-start
  1.4 1.2 %copy-done = bf16[1,4,1024,128]{3,2,1,0:T(8,128)(2,1)S(1)} copy-done((bf16[1,4,1024,128]{3,2,1,0:T(8,128)(2,1)S(1)}, bf16[1,4,1024,128]{3,2,1,0:T(8,128)(2,1)}, u32[]{:S(2)}) %copy-start) | copy-done | bytes 1048600
  2.6 0.0 copy-start.2
  2.6 0.9 %copy-done.2 = bf16[4,128,128]{2,1,0:T(8,128)(2,1)S(1)} copy-done((bf16[4,128,128]{2,1,0:T(8,128)(2,1)S(1)}, bf16[4,128,128]{2,1,0:T(8,128)(2,1)}, u32[]{:S(2)}) %copy-start.2) | copy-done | bytes 131096
  3.5 0.0 copy-start.3
  3.5 0.9 %copy-done.3 = bf16[4,128,128]{2,1,0:T(8,128)(2,1)S(1)} copy-done((bf16[4,128,128]{2,1,0:T(8,128)(2,1)S(1)}, bf16[4,128,128]{2,1,0:T(8,128)(2,1)}, u32[]{:S(2)}) %copy-start.3) | copy-done | bytes 131096
  4.4 0.0 copy-start.4
  4.4 0.8 %copy-done.4 = bf16[1,256,128]{2,1,0:T(8,128)(2,1)S(1)} copy-done((bf16[1,256,128]{2,1,0:T(8,128)(2,1)S(1)}, bf16[1,256,128]{2,1,0:T(8,128)(2,1)}, u32[]{:S(2)}) %copy-start.4) | copy-done | bytes 65560
  5.2 0.0 copy-start.5
  5.2 0.8 %copy-done.5 = bf16[1,256,128]{2,1,0:T(8,128)(2,1)S(1)} copy-done((bf16[1,256,128]{2,1,0:T(8,128)(2,1)S(1)}, bf16[1,256,128]{2,1,0:T(8,128)(2,1)}, u32[]{:S(2)}) %copy-start.5) | copy-done | bytes 65560
  6.1 0.0 copy-start.1
  6.1 24.5 %factor.1 = (bf16[8,4,128,128]{3,2,1,0:T(8,128)(2,1)S(1)}, bf16[4,1024,128]{2,1,0:T(8,128)(2,1)S(1)}, bf16[4,256,128]{2,1,0:T(8,128)(2,1)S(1)}, bf16[4,2,256,128]{3,2,1,0:T(8,128)(2,1)S(1)}) custom-call(s32[1,4]{1,0:T(1,128)S(1)} %copy-done.6, s32[4]{0:T(128)S(1)} %copy-done.7, s32[1]{0:T(128)S(6)} %copy.12.row_rank, s32[1,4]{1,0:T(1,128)S(1)} %copy-done.8, ...), custom_call_target="tpu_custom_call" | custom-call | tf_op jit(solution)/shard_map/factor/pallas_call | solution.py:408
  30.6 0.0 copy-done.1
  30.6 3.3 %product.1 = (bf16[1,4,1024,128]{3,2,1,0:T(8,128)(2,1)}, bf16[1,4,1024,128]{3,2,1,0:T(8,128)(2,1)}) custom-call(bf16[4,1024,128]{2,1,0:T(8,128)(2,1)S(1)} %get-tuple-element.6.left, bf16[4,256,128]{2,1,0:T(8,128)(2,1)S(1)} %get-tuple-element.7.u_parts, bf16[1,4,1024,128]{3,2,1,0:T(8,128)(2,1)S(1)} %copy-done.1, ...), custom_call_target="tpu_custom_call" | custom-call | tf_op jit(solution)/shard_map/product/pallas_call | solution.py:456
Async XLA Ops:
  0.6 0.7 %copy-start.8 = (s32[1,4]{1,0:T(1,128)S(1)}, s32[1,4]{1,0:T(1,128)}, u32[]{:S(2)}) copy-start(s32[1,4]{1,0:T(1,128)} %target_rank.1) | copy-start | bytes 52
  0.6 0.7 %copy-start.7 = (s32[4]{0:T(128)S(1)}, s32[4]{0:T(128)}, u32[]{:S(2)}) copy-start(s32[4]{0:T(128)} %band_rank.1) | copy-start | bytes 52
  0.7 0.7 %copy-start.6 = (s32[1,4]{1,0:T(1,128)S(1)}, s32[1,4]{1,0:T(1,128)}, u32[]{:S(2)}) copy-start(s32[1,4]{1,0:T(1,128)} %tile_rank.1) | copy-start | bytes 52
  1.4 1.2 %copy-start = (bf16[1,4,1024,128]{3,2,1,0:T(8,128)(2,1)S(1)}, bf16[1,4,1024,128]{3,2,1,0:T(8,128)(2,1)}, u32[]{:S(2)}) copy-start(bf16[1,4,1024,128]{3,2,1,0:T(8,128)(2,1)} %tile_u.1) | copy-start | bytes 3145732
  2.6 0.9 %copy-start.2 = (bf16[4,128,128]{2,1,0:T(8,128)(2,1)S(1)}, bf16[4,128,128]{2,1,0:T(8,128)(2,1)}, u32[]{:S(2)}) copy-start(bf16[4,128,128]{2,1,0:T(8,128)(2,1)} %pu.1) | copy-start | bytes 393220
  3.5 0.9 %copy-start.3 = (bf16[4,128,128]{2,1,0:T(8,128)(2,1)S(1)}, bf16[4,128,128]{2,1,0:T(8,128)(2,1)}, u32[]{:S(2)}) copy-start(bf16[4,128,128]{2,1,0:T(8,128)(2,1)} %pv.1) | copy-start | bytes 393220
  4.4 0.8 %copy-start.4 = (bf16[1,256,128]{2,1,0:T(8,128)(2,1)S(1)}, bf16[1,256,128]{2,1,0:T(8,128)(2,1)}, u32[]{:S(2)}) copy-start(bf16[1,256,128]{2,1,0:T(8,128)(2,1)} %ru.1) | copy-start | bytes 196612
  5.2 0.8 %copy-start.5 = (bf16[1,256,128]{2,1,0:T(8,128)(2,1)S(1)}, bf16[1,256,128]{2,1,0:T(8,128)(2,1)}, u32[]{:S(2)}) copy-start(bf16[1,256,128]{2,1,0:T(8,128)(2,1)} %rv.1) | copy-start | bytes 196612
  6.1 24.5 %copy-start.1 = (bf16[1,4,1024,128]{3,2,1,0:T(8,128)(2,1)S(1)}, bf16[1,4,1024,128]{3,2,1,0:T(8,128)(2,1)}, u32[]{:S(2)}) copy-start(bf16[1,4,1024,128]{3,2,1,0:T(8,128)(2,1)} %tile_v.1) | copy-start | bytes 3145732

commit v3 on v2

--- a/solution.py
+++ b/solution.py
@@ -270,7 +270,7 @@
 def factor_kernel(
     n_blk, n_col, tile_rank, band_rank, row_rank, target_rank, tile_u, ru, rv, pu, pv,
     all_pu, left_out, u_out, v_out,
-    tu, all_ru, all_rv, all_pv, left, work, gram_t, gram_r, cores,
+    tu, own_ru, near_ru, far_ru, all_ru, all_rv, all_pv, left, work, gram_t, gram_r, cores,
     own_sem, tile_sem, left_sem, col_send, col_recv, blk_send, blk_recv, pair_send, pair_recv,
 ):
     tiles, order, width = tu.shape
@@ -280,7 +280,7 @@
     near = {step: flip(group, step) * 2 + side for step in (1, 2, 3)}
 
     locals_ = [
-        pltpu.make_async_copy(ru.at[0], all_ru.at[c], own_sem.at[0]),
+        pltpu.make_async_copy(ru.at[0], own_ru, own_sem.at[0]),
         pltpu.make_async_copy(rv.at[0], all_rv.at[c], own_sem.at[1]),
         pltpu.make_async_copy(pv, all_pv.at[b], own_sem.at[2]),
         pltpu.make_async_copy(pu, all_pu.at[b], own_sem.at[3]),
@@ -291,6 +291,26 @@
     for copy in locals_ + tile_copies:
         copy.start()
 
+    chunk = order // n_col
+    part, half = chunk // 2, width // 2
+    row = lax.broadcasted_iota(jnp.int32, (width, width), 0)
+    col = lax.broadcasted_iota(jnp.int32, (width, width), 1)
+    place = col // 2
+    even = col % 2 == 0
+
+    def one_hot(*blocks):
+        return jnp.concatenate([block.astype(BF16) for block in blocks], axis=0)
+
+    locals_[0].wait()
+    mine = jnp.concatenate([own_ru[:part, :], own_ru[part:, :]], axis=1)
+    low = col < half
+    for whole, shift in ((near_ru, 0), (far_ru, half)):
+        whole[c] = jnp.dot(
+            mine,
+            one_hot((row == col + shift) & low, (row == col - half + shift) & jnp.logical_not(low)),
+            preferred_element_type=F32,
+        ).astype(BF16)
+
     barrier = pltpu.get_barrier_semaphore()
     peers = [(b, (c + step) % n_col) for step in range(1, n_col)]
     peers += [(near[1], c), (near[2], c), (sibling, c)]
@@ -301,7 +321,7 @@
     def row_sends(at, source, whole):
         copies = [
             pltpu.make_async_remote_copy(
-                src_ref=source.at[0],
+                src_ref=source,
                 dst_ref=whole.at[c],
                 send_sem=col_send.at[at, step],
                 recv_sem=col_recv.at[at, step],
@@ -326,7 +346,7 @@
         copy.start()
         return copy
 
-    ru_copies = row_sends(0, ru, all_ru)
+    near_copies = row_sends(0, near_ru.at[c], near_ru)
     wholes = (all_pv, all_pu)
     blk_copies, pair_copies = {}, []
     for at, source in enumerate((pv, pu)):
@@ -351,41 +371,77 @@
             panel_send(at, step, here, wholes[at], slot, sibling, pair_send, pair_recv)
         )
 
-    locals_[0].wait()
-    for copy in ru_copies:
+    for copy in near_copies:
         copy.wait_recv()
-    rv_copies = row_sends(1, rv, all_rv)
-    ru_all = all_ru[...].reshape(order, width)
+    far_copies = row_sends(1, far_ru.at[c], far_ru)
+    rv_copies = row_sends(2, rv.at[0], all_rv)
     rr = row_rank[0]
     left_copies = []
     for t in range(tiles):
+        tr = tile_rank[0, t]
         tile_copies[t].wait()
-        first_half(t, tu[t], ru_all, tile_rank[0, t], rr, left, gram_t, gram_r, work)
-        if t == tiles // 2 - 1:
-            for at, step in ((0, 2), (1, 1), (0, 1), (1, 2)):
-                pass_on(at, step)
+        pick_t = (row == place) & even & (row < tr)
+        for side_by in range(2):
+            pick_r = (row - side_by * half == place) & jnp.logical_not(even) & (place < rr)
+            starts = [q * chunk + side_by * part for q in range(n_col)]
+            both = jnp.concatenate(
+                [
+                    jnp.concatenate([tu[t, start : start + part, :], near_ru[q]], axis=1)
+                    for q, start in enumerate(starts)
+                ],
+                axis=0,
+            )
+            first = jnp.dot(both, one_hot(pick_t, pick_r), preferred_element_type=F32)
+            first = first.astype(BF16)
+            for q, start in enumerate(starts):
+                left[t, start : start + part, :] = first[q * part : (q + 1) * part]
+        first = left[t]
+        spare = (row == col) & (place >= jnp.where(even, tr, rr))
+        work[pl.ds(t, width, stride=SUB), :] = across(first, first) + spare.astype(F32)
     for t in range(tiles):
         copy = pltpu.make_async_copy(left.at[t], left_out.at[t], left_sem.at[t])
         copy.start()
         left_copies.append(copy)
 
+    def neighbours():
+        for at, step in ((0, 2), (1, 1), (0, 1), (1, 2)):
+            pass_on(at, step)
+        for t in range(tiles):
+            gram_t[t] = across(tu[t], left[t])
+
+    def row_grams():
+        for copy in far_copies:
+            copy.wait_recv()
+        for side_by in range(2):
+            back = one_hot(
+                (row - side_by * half == col) & low,
+                (row - side_by * half == col - half) & jnp.logical_not(low),
+            )
+            for q in range(n_col):
+                both = jnp.concatenate([near_ru[q], far_ru[q]], axis=1)
+                start = q * chunk + side_by * part
+                all_ru[start : start + part, :] = jnp.dot(
+                    both, back, preferred_element_type=F32
+                ).astype(BF16)
+        for t in range(tiles):
+            gram_r[t] = across(all_ru[...], left[t])
+
     def diagonal():
         pass_on(0, 3)
         pass_on(1, 3)
 
-    def cores_ready():
-        row = lax.broadcasted_iota(jnp.int32, (width, width), 0)
-        for copy in locals_[1:]:
-            copy.wait()
-        for copy in rv_copies + pair_copies:
-            copy.wait_recv()
-        rv_all = all_rv[...].reshape(order, width)
-        for t in range(tiles):
-            cores[t] = jnp.where(
-                row < rr, across(rv_all, all_pv[:, t].reshape(order, width)), 0.0
-            )
-
-    eliminate(work, width, tiles, {SUPER: diagonal, 3 * SUPER: cores_ready})
+    eliminate(
+        work, width, tiles, {SUPER: neighbours, 2 * SUPER: row_grams, 3 * SUPER: diagonal}
+    )
+    for copy in locals_[1:]:
+        copy.wait()
+    for copy in rv_copies + pair_copies:
+        copy.wait_recv()
+    rv_all = all_rv[...].reshape(order, width)
+    for t in range(tiles):
+        cores[t] = jnp.where(
+            row < rr, across(rv_all, all_pv[:, t].reshape(order, width)), 0.0
+        )
     for t in range(tiles):
         ranks = (tile_rank[0, t], band_rank[t], target_rank[0, t])
         u_parts, v_parts = factors(t, math.sqrt(order), ranks, cores[t], gram_t, gram_r, work)
@@ -393,7 +449,7 @@
         v_out[t, 0], v_out[t, 1] = v_parts
     for copy in left_copies:
         copy.wait()
-    for copy in ru_copies + rv_copies + list(blk_copies.values()) + pair_copies:
+    for copy in near_copies + far_copies + rv_copies + list(blk_copies.values()) + pair_copies:
         copy.wait_send()
 
 
@@ -405,6 +461,7 @@
     dma = pltpu.SemaphoreType.DMA
     row_shape = (n_col,) + row_u.shape[1:]
     panel_shape = (n_blk,) + panel_u.shape
+    packed = (n_col, row_u.shape[1] // 2, width)
     return pl.pallas_call(
         functools.partial(factor_kernel, n_blk, n_col),
         out_shape=[
@@ -413,11 +470,14 @@
             jax.ShapeDtypeStruct((tiles, 2 * width, width), BF16),
             jax.ShapeDtypeStruct((tiles, 2, 2 * width, width), BF16),
         ],
-        in_specs=[smem] * 4 + [any_space] * 5,
+        in_specs=[smem] * 4 + [pl.BlockSpec(memory_space=pltpu.HBM)] * 5,
         out_specs=[any_space] * 2 + [vmem] * 2,
         scratch_shapes=[
             pltpu.VMEM((tiles, order, width), BF16),
-            pltpu.VMEM(row_shape, BF16),
+            pltpu.VMEM(row_u.shape[1:], BF16),
+            pltpu.VMEM(packed, BF16),
+            pltpu.VMEM(packed, BF16),
+            pltpu.VMEM((order, width), BF16),
             pltpu.VMEM(row_shape, BF16),
             pltpu.VMEM(panel_shape, BF16),
             pltpu.VMEM((tiles, order, width), BF16),
@@ -428,15 +488,15 @@
             dma((4,)),
             dma((tiles,)),
             dma((tiles,)),
-            dma((2, n_col)),
-            dma((2, n_col)),
+            dma((3, n_col)),
+            dma((3, n_col)),
             dma((2, 4)),
             dma((2, 4)),
             dma((2, 4)),
             dma((2, 4)),
         ],
         compiler_params=pltpu.CompilerParams(
-            collective_id=0, has_side_effects=True, vmem_limit_bytes=32 * 1024 * 1024
+            collective_id=0, has_side_effects=True, vmem_limit_bytes=60 * 1024 * 1024
         ),
         name="factor",
     )(tile_rank, band_rank, row_rank, target_rank, tile_u, row_u, row_v, panel_u, panel_v)
@@ -465,7 +525,7 @@
             pl.BlockSpec((1, 2, 2 * width, width), lambda t: (t, 0, 0, 0)),
         ],
         out_specs=[tile] * 2,
-        compiler_params=pltpu.CompilerParams(vmem_limit_bytes=32 * 1024 * 1024),
+        compiler_params=pltpu.CompilerParams(vmem_limit_bytes=60 * 1024 * 1024),
         name="product",
     )(left, u_parts, tile_v, all_pu, v_parts)
 

time: 34.1 us -> 30.5 us (0.89)
  local copies, waits for them, and re-layouts: 4.72 us -> 0 us
  Pallas kernels: 27.7 us -> 28.9 us
    unnamed x18 -> x0, local copies, waits for them, and re-layouts: 4.72 us -> none
    pallas_call x1, Pallas kernels: 3.25 us -> 5.02 us  [product(): pl.pallas_call(product_kernel, grid=(tiles,), out_shape=[jax.ShapeDtypeSt...]
    pallas_call x1, Pallas kernels: 24.5 us -> 23.8 us  [factor(): pl.pallas_call(functools.partial(factor_kernel, n_blk, n_col), out_shape=...]
where the time goes in v3:
time: 30.5 us; the launch traced here: 30.2 us
  Pallas kernels  28.9 us (95%)
  between operations  1.29 us (4%)
    pallas_call x1, Pallas kernels, factor(): pl.pallas_call(functools.partial(factor_kernel, n_blk, n_col), out_shape=...  23.8 us
    pallas_call x1, Pallas kernels, product(): pl.pallas_call(product_kernel, grid=(tiles,), out_shape=[jax.ShapeDtypeSt...  5.02 us

profile of v3, /device:TPU:0, one launch (start us, length us, event | category | flops | bytes accessed | tf_op | source)
XLA Modules:
  0.0 30.2 jit_solution(8083757695887046930)
XLA Ops:
  1.3 23.8 %factor.1 = (bf16[8,4,128,128]{3,2,1,0:T(8,128)(2,1)}, bf16[4,1024,128]{2,1,0:T(8,128)(2,1)}, bf16[4,256,128]{2,1,0:T(8,128)(2,1)}, bf16[4,2,256,128]{3,2,1,0:T(8,128)(2,1)}) custom-call(s32[1,4]{1,0:T(1,128)} %tile_rank.1, s32[4]{0:T(128)} %band_rank.1, s32[1]{0:T(128)S(6)} %copy.12.row_rank, s32[1,4]{1,0:T(1,128)} %target_rank.1, ...), custom_call_target="tpu_custom_call" | custom-call | tf_op jit(solution)/shard_map/factor/pallas_call | solution.py:465
  25.1 5.0 %product.1 = (bf16[1,4,1024,128]{3,2,1,0:T(8,128)(2,1)}, bf16[1,4,1024,128]{3,2,1,0:T(8,128)(2,1)}) custom-call(bf16[4,1024,128]{2,1,0:T(8,128)(2,1)} %get-tuple-element.6.left, bf16[4,256,128]{2,1,0:T(8,128)(2,1)} %get-tuple-element.7.u_parts, bf16[1,4,1024,128]{3,2,1,0:T(8,128)(2,1)} %tile_v.1, bf16[8,4,128,128]{3,2,1,0:T(8,128)(2,1)} %get-tuple-element.8.all_pu, ...), custom_call_target="tpu_custom_call" | custom-call | tf_op jit(solution)/shard_map/product/pallas_call | solution.py:516

commit v4 on v3

--- a/solution.py
+++ b/solution.py
@@ -8,7 +8,6 @@
 from jax.experimental.pallas import tpu as pltpu
 from jax.sharding import PartitionSpec as P
 
-HIGH = lax.Precision.HIGHEST
 MESH = pl.DeviceIdType.MESH
 F32 = jnp.float32
 BF16 = jnp.bfloat16
@@ -136,9 +135,9 @@
     )(row_u, row_v, panel_u, panel_v)
 
 
-def across(first, second, precision=None):
+def across(first, second):
     return lax.dot_general(
-        first, second, (((0,), (0,)), ((), ())), precision=precision, preferred_element_type=F32
+        first, second, (((0,), (0,)), ((), ())), preferred_element_type=F32
     )
 
 
@@ -168,9 +167,10 @@
     col = lax.broadcasted_iota(jnp.int32, (width, width), 1)
     inverse = jnp.where(col <= row, work[pl.ds(t, width, stride=SUB), :], 0.0).T
     inverse = jnp.where(col < tk, inverse, 0.0)
-    head_t = jnp.dot(gram_t[t], inverse, precision=HIGH, preferred_element_type=F32)
-    head_r = jnp.dot(gram_r[t], inverse, precision=HIGH, preferred_element_type=F32)
-    panel = across(core, head_r, HIGH)
+    grams = jnp.concatenate([gram_t[t], gram_r[t]], axis=0)
+    heads = jnp.dot(*stacked(grams, inverse, 1, 0), preferred_element_type=F32)
+    head_t, head_r = heads[:width], heads[width:]
+    panel = across(*stacked(core, head_r, 0, 0))
     head_t = jnp.where(row < tr, head_t, 0.0) / scale
     panel = jnp.where(row < br, -panel, 0.0) / scale
     return split(inverse * scale), split(jnp.concatenate([head_t, panel], axis=0))
@@ -179,6 +179,20 @@
 def split(value):
     high = value.astype(BF16)
     return high, (value - high.astype(F32)).astype(BF16)
+
+
+def stacked(first, second, first_axis, second_axis):
+    parts = []
+    for value in (first, second):
+        a = value.astype(BF16)
+        rest = value - a.astype(F32)
+        b = rest.astype(BF16)
+        parts.append((a, b, (rest - b.astype(F32)).astype(BF16)))
+    (a, b, c), (d, e, f) = parts
+    return (
+        jnp.concatenate([a, a, b, b, a, c], axis=first_axis),
+        jnp.concatenate([d, e, d, e, f, d], axis=second_axis),
+    )
 
 
 def eliminate(work, width, tiles, between={}):
@@ -225,7 +239,7 @@
             ahead = (ahead > pivot) & (ahead < below)
             for t in range(tiles):
                 pivots = work[pl.ds(top * SUB + t, SUPER, stride=SUB), :]
-                update = across(pivots, jnp.where(ahead, 0.0, pivots), HIGH)[below:, :]
+                update = across(*stacked(pivots, jnp.where(ahead, 0.0, pivots), 0, 0))[below:, :]
                 old = work[pl.ds(below * SUB + t, rest, stride=SUB), :]
                 work[pl.ds(below * SUB + t, rest, stride=SUB), :] = (
                     jnp.where(done, 0.0, old) - update
@@ -279,6 +293,12 @@
     sibling = group * 2 + 1 - side
     near = {step: flip(group, step) * 2 + side for step in (1, 2, 3)}
 
+    barrier = pltpu.get_barrier_semaphore()
+    peers = [(b, (c + step) % n_col) for step in range(1, n_col)]
+    peers += [(near[1], c), (near[2], c), (sibling, c)]
+    for peer in peers:
+        pl.semaphore_signal(barrier, inc=1, device_id=peer, device_id_type=MESH)
+
     locals_ = [
         pltpu.make_async_copy(ru.at[0], own_ru, own_sem.at[0]),
         pltpu.make_async_copy(rv.at[0], all_rv.at[c], own_sem.at[1]),
@@ -291,31 +311,6 @@
     for copy in locals_ + tile_copies:
         copy.start()
 
-    chunk = order // n_col
-    part, half = chunk // 2, width // 2
-    row = lax.broadcasted_iota(jnp.int32, (width, width), 0)
-    col = lax.broadcasted_iota(jnp.int32, (width, width), 1)
-    place = col // 2
-    even = col % 2 == 0
-
-    def one_hot(*blocks):
-        return jnp.concatenate([block.astype(BF16) for block in blocks], axis=0)
-
-    locals_[0].wait()
-    mine = jnp.concatenate([own_ru[:part, :], own_ru[part:, :]], axis=1)
-    low = col < half
-    for whole, shift in ((near_ru, 0), (far_ru, half)):
-        whole[c] = jnp.dot(
-            mine,
-            one_hot((row == col + shift) & low, (row == col - half + shift) & jnp.logical_not(low)),
-            preferred_element_type=F32,
-        ).astype(BF16)
-
-    barrier = pltpu.get_barrier_semaphore()
-    peers = [(b, (c + step) % n_col) for step in range(1, n_col)]
-    peers += [(near[1], c), (near[2], c), (sibling, c)]
-    for peer in peers:
-        pl.semaphore_signal(barrier, inc=1, device_id=peer, device_id_type=MESH)
     pl.semaphore_wait(barrier, len(peers))
 
     def row_sends(at, source, whole):
@@ -346,7 +341,6 @@
         copy.start()
         return copy
 
-    near_copies = row_sends(0, near_ru.at[c], near_ru)
     wholes = (all_pv, all_pu)
     blk_copies, pair_copies = {}, []
     for at, source in enumerate((pv, pu)):
@@ -358,6 +352,28 @@
         pair_copies.append(
             panel_send(at, 0, source, wholes[at], b, sibling, pair_send, pair_recv)
         )
+
+    chunk = order // n_col
+    part, half = chunk // 2, width // 2
+    row = lax.broadcasted_iota(jnp.int32, (width, width), 0)
+    col = lax.broadcasted_iota(jnp.int32, (width, width), 1)
+    place = col // 2
+    even = col % 2 == 0
+
+    def one_hot(*blocks):
+        return jnp.concatenate([block.astype(BF16) for block in blocks], axis=0)
+
+    locals_[0].wait()
+    mine = jnp.concatenate([own_ru[:part, :], own_ru[part:, :]], axis=1)
+    low = col < half
+    for whole, shift in ((near_ru, 0), (far_ru, half)):
+        whole[c] = jnp.dot(
+            mine,
+            one_hot((row == col + shift) & low, (row == col - half + shift) & jnp.logical_not(low)),
+            preferred_element_type=F32,
+        ).astype(BF16)
+
+    near_copies = row_sends(0, near_ru.at[c], near_ru)
 
     def pass_on(at, step):
         blk_copies[at, step].wait_recv()
@@ -511,18 +527,18 @@
 
 def product(left, u_parts, tile_v, all_pu, v_parts):
     tiles, order, width = left.shape
-    tile = pl.BlockSpec((1, 1, order, width), lambda t: (0, t, 0, 0))
+    tile = pl.BlockSpec((1, 1, order // 2, width), lambda t, h: (0, t, h, 0))
     n_blk, _, rows, _ = all_pu.shape
     return pl.pallas_call(
         product_kernel,
-        grid=(tiles,),
+        grid=(tiles, 2),
         out_shape=[jax.ShapeDtypeStruct(tile_v.shape, BF16)] * 2,
         in_specs=[
-            pl.BlockSpec((1, order, width), lambda t: (t, 0, 0)),
-            pl.BlockSpec((1, 2 * width, width), lambda t: (t, 0, 0)),
+            pl.BlockSpec((1, order // 2, width), lambda t, h: (t, h, 0)),
+            pl.BlockSpec((1, 2 * width, width), lambda t, h: (t, 0, 0)),
             tile,
-            pl.BlockSpec((n_blk, 1, rows, width), lambda t: (0, t, 0, 0)),
-            pl.BlockSpec((1, 2, 2 * width, width), lambda t: (t, 0, 0, 0)),
+            pl.BlockSpec((n_blk // 2, 1, rows, width), lambda t, h: (h, t, 0, 0)),
+            pl.BlockSpec((1, 2, 2 * width, width), lambda t, h: (t, 0, 0, 0)),
         ],
         out_specs=[tile] * 2,
         compiler_params=pltpu.CompilerParams(vmem_limit_bytes=60 * 1024 * 1024),

time: 30.5 us -> 32 us (1.049)
  Pallas kernels: 28.9 us -> 30.3 us
    pallas_call x1, Pallas kernels: 5.02 us -> 7.35 us  [product(): pl.pallas_call(product_kernel, grid=(tiles, 2), out_shape=[jax.ShapeDtype...]
    pallas_call x1, Pallas kernels: 23.8 us -> 23 us  [factor(): pl.pallas_call(functools.partial(factor_kernel, n_blk, n_col), out_shape=...]
where the time goes in v4:
time: 32 us; the launch traced here: 31.6 us
  Pallas kernels  30.3 us (95%)
  between operations  1.29 us (4%)
    pallas_call x1, Pallas kernels, factor(): pl.pallas_call(functools.partial(factor_kernel, n_blk, n_col), out_shape=...  23 us
    pallas_call x1, Pallas kernels, product(): pl.pallas_call(product_kernel, grid=(tiles, 2), out_shape=[jax.ShapeDtype...  7.35 us

profile of v4, /device:TPU:0, one launch (start us, length us, event | category | flops | bytes accessed | tf_op | source)
XLA Modules:
  0.0 31.6 jit_solution(3708397816911830310)
XLA Ops:
  1.3 23.0 %factor.1 = (bf16[8,4,128,128]{3,2,1,0:T(8,128)(2,1)}, bf16[4,1024,128]{2,1,0:T(8,128)(2,1)}, bf16[4,256,128]{2,1,0:T(8,128)(2,1)}, bf16[4,2,256,128]{3,2,1,0:T(8,128)(2,1)}) custom-call(s32[1,4]{1,0:T(1,128)} %tile_rank.1, s32[4]{0:T(128)} %band_rank.1, s32[1]{0:T(128)S(6)} %copy.12.row_rank, s32[1,4]{1,0:T(1,128)} %target_rank.1, ...), custom_call_target="tpu_custom_call" | custom-call | tf_op jit(solution)/shard_map/factor/pallas_call | solution.py:481
  24.2 7.4 %product.1 = (bf16[1,4,1024,128]{3,2,1,0:T(8,128)(2,1)}, bf16[1,4,1024,128]{3,2,1,0:T(8,128)(2,1)}) custom-call(bf16[4,1024,128]{2,1,0:T(8,128)(2,1)} %get-tuple-element.6.left, bf16[4,256,128]{2,1,0:T(8,128)(2,1)} %get-tuple-element.7.u_parts, bf16[1,4,1024,128]{3,2,1,0:T(8,128)(2,1)} %tile_v.1, bf16[8,4,128,128]{3,2,1,0:T(8,128)(2,1)} %get-tuple-element.8.all_pu, ...), custom_call_target="tpu_custom_call" | custom-call | tf_op jit(solution)/shard_map/product/pallas_call | solution.py:532
